TPU v7x, 1024 devices: a whole 4x4x32 slice. The times are simulated.
1024 devices in a mesh: dp: 64 (over z_lo, x, core), mp: 16 (over z_hi, y).
Axes of the slice: x: 4, y: 4, z: 32 (z_hi: 4, z_lo: 8; z = z_hi * 8 + z_lo), core: 2. Of those that a mesh axis runs over, the one named last changes fastest.
Arguments:
- inputs: bfloat16 [2048, 6144], P('dp', 'mp'), may hold values from -6 to 6
- act_grad: bfloat16 [2048, 24576], P('mp', 'dp'), may hold values from -6 to 6
- w_in: bfloat16 [6144, 24576], P('mp', 'dp'), may hold values from -0.078125 to 0.078125
- bias_in: float32 [24576], P('dp'), may hold values from -5 to 5
Outputs:
- input_grad: bfloat16 [2048, 6144], P('dp', 'mp')
- w_in_grad: float32 [6144, 24576], P('mp', 'dp')
- bias_grad: float32 [24576], P('dp')
All inputs are finite; a program needn't handle non-finite values.
Results may differ from a plain program's by a relative error of at most 0.017.
Values may be sent and summed in bfloat16 or wider, within the bound.
A program may use at most 32 MiB of HBM per device.

v0:
```python
import math

import jax
import jax.numpy as jnp
from jax import lax
from jax.sharding import PartitionSpec as P


def gelu_slope(pre):
    cdf = 0.5 * (1.0 + jax.scipy.special.erf(pre * (1.0 / math.sqrt(2.0))))
    dens = jnp.exp(-0.5 * pre * pre) * (1.0 / math.sqrt(2.0 * math.pi))
    return cdf + pre * dens


def contract(left, right, left_dim, right_dim):
    return lax.dot_general(
        left, right, (((left_dim,), (right_dim,)), ((), ())), preferred_element_type=jnp.float32
    )


def body(inputs, act_grad, w_in, bias_in):
    all_inputs = lax.all_gather(inputs, "dp", axis=0, tiled=True)
    pre = (
        lax.psum_scatter(
            contract(all_inputs, w_in, 1, 0).astype(jnp.bfloat16),
            "mp",
            scatter_dimension=0,
            tiled=True,
        ).astype(jnp.float32)
        + bias_in
    )
    hidden_grad = (act_grad.astype(jnp.float32) * gelu_slope(pre)).astype(jnp.bfloat16)
    all_grad = lax.all_gather(hidden_grad, "mp", axis=0, tiled=True)
    w_in_grad = contract(all_inputs, all_grad, 0, 0)
    bias_grad = jnp.sum(all_grad, axis=0, dtype=jnp.float32)
    input_grad = lax.psum_scatter(
        contract(all_grad, w_in, 1, 1), "dp", scatter_dimension=0, tiled=True
    ).astype(jnp.bfloat16)
    return (input_grad, w_in_grad, bias_grad)


def solution(mesh):
    return jax.shard_map(
        body,
        mesh=mesh,
        in_specs=(P("dp", "mp"), P("mp", "dp"), P("mp", "dp"), P("dp")),
        out_specs=(P("dp", "mp"), P("mp", "dp"), P("dp")),
        check_vma=False,
    )
```

profile of v0, /device:TPU:1, one launch (start us, length us, event | category | flops | bytes accessed | tf_op | source)
XLA Modules:
  0.0 943.0 jit_solution(3991516490588693587)
XLA Ops:
  7.2 0.0 copy-start
  7.2 0.0 all-gather.3.cloned.1.call-start
  7.2 0.7 all-gather.3.cloned.1.call-update
  7.9 0.0 reduce-scatter.3.cloned.1.call-start
  8.0 142.1 %all-gather.3.cloned.1.call-done = bf16[2048,384]{1,0:T(8,128)(2,1)} async-done(((bf16[32,384]{1,0:T(8,128)(2,1)}), bf16[2048,384]{1,0:T(8,128)(2,1)}) %all-gather.3.cloned.1.call-update) | async-done | bytes 1572880 | tf_op jit(solution)/shard_map/all_gather | solution.py:22
  150.1 0.0 copy-done
  150.1 3.7 convolution_convert_fusion
  153.8 0.0 reduce-scatter.3.cloned.1.call-update
  153.8 0.0 all-gather.5.cloned.1.call-start
  153.8 200.6 %reduce-scatter.3.cloned.1.call-done = bf16[128,384]{1,0:T(8,128)(2,1)} async-done(((bf16[2048,384]{1,0:T(8,128)(2,1)}), bf16[128,384]{1,0:T(8,128)(2,1)}) %reduce-scatter.3.cloned.1.call-update) | async-done | bytes 98320 | tf_op jit(solution)/shard_map/reduce_scatter | solution.py:24
  354.5 0.0 copy-done.3
  354.5 1.6 fusion.5
  356.1 0.0 all-gather.5.cloned.1.call-update
  356.2 0.0 reduce-scatter.5.cloned.1.call-start
  356.2 144.7 %all-gather.5.cloned.1.call-done = bf16[2048,384]{1,0:T(8,128)(2,1)} async-done(((bf16[128,384]{1,0:T(8,128)(2,1)}), bf16[2048,384]{1,0:T(8,128)(2,1)}) %all-gather.5.cloned.1.call-update) | async-done | bytes 1572880 | tf_op jit(solution)/shard_map/all_gather | solution.py:33
  500.9 4.2 fusion.6
  505.0 0.0 reduce-scatter.5.cloned.1.call-update
  505.1 1.4 copy-done.1
  506.4 0.5 copy-done.2
  506.9 1.8 convolution_bitcast_fusion
  508.8 2.1 copy.7
  510.9 0.9 convert_reduce_fusion
  511.7 423.3 %reduce-scatter.5.cloned.1.call-done = f32[32,384]{1,0:T(8,128)} async-done(((f32[2048,384]{1,0:T(8,128)}), f32[32,384]{1,0:T(8,128)}) %reduce-scatter.5.cloned.1.call-update) | async-done | bytes 49168 | tf_op jit(solution)/shard_map/reduce_scatter | solution.py:36
  935.1 1.4 convert_element_type.22
  (5 shorter events, 0.0 us)
Async XLA Ops:
  7.2 142.9 %copy-start = (bf16[384,384]{1,0:T(8,128)(2,1)S(1)}, bf16[384,384]{1,0:T(8,128)(2,1)}, u32[]{:S(2)}) copy-start(bf16[384,384]{1,0:T(8,128)(2,1)} %param.6) | copy-start | bytes 884740
  7.2 142.9 %all-gather.3.cloned.1.call-start = ((), (), s32[]{:S(2)}) async-start(), calls=%async_computation.2 | async-start | bytes 1597440 | tf_op jit(solution)/shard_map/all_gather | solution.py:22
  7.9 346.6 %reduce-scatter.3.cloned.1.call-start = ((), (), s32[]{:S(2)}) async-start(), calls=%async_computation.3 | async-start | bytes 1671168 | tf_op jit(solution)/shard_map/reduce_scatter | solution.py:24
  153.8 200.7 %copy-start.3 = (bf16[128,384]{1,0:T(8,128)(2,1)S(1)}, bf16[128,384]{1,0:T(8,128)(2,1)}, u32[]{:S(2)}) copy-start(bf16[128,384]{1,0:T(8,128)(2,1)} %param.5) | copy-start | bytes 294916
  153.8 200.7 %copy-start.4 = (f32[384]{0:T(512)S(1)}, f32[384]{0:T(512)}, u32[]{:S(2)}) copy-start(f32[384]{0:T(512)} %param.7) | copy-start | bytes 4612
  153.8 347.1 %all-gather.5.cloned.1.call-start = ((), (), s32[]{:S(2)}) async-start(), calls=%async_computation.4 | async-start | bytes 1671168 | tf_op jit(solution)/shard_map/all_gather | solution.py:33
  356.2 578.9 %reduce-scatter.5.cloned.1.call-start = ((), (), s32[]{:S(2)}) async-start(), calls=%async_computation.5 | async-start | bytes 3194880 | tf_op jit(solution)/shard_map/reduce_scatter | solution.py:36
  505.0 1.4 copy-start.1
  505.0 1.9 copy-start.2
Sparse Core Ops, SparseCore 0:
  10.7 139.2 all-gather.2
  155.3 199.0 reduce-scatter.2
  359.2 141.5 all-gather.4
  505.2 429.8 reduce-scatter.4
where the time goes:
time: 951 us; the launch traced here: 943 us
  waiting for transfers between devices  912 us (96%)
  between operations  13.8 us (1%)
  matrix products  9.67 us (1%)
    reduce_scatter x1, waiting for transfers between devices, body(): lax.psum_scatter(contract(all_grad, w_in, 1, 1), 'dp', scatter_dimension=...  423 us
    reduce_scatter x1, waiting for transfers between devices, body(): lax.psum_scatter(contract(all_inputs, w_in, 1, 0).astype(jnp.bfloat16), '...  201 us
    all_gather x1, waiting for transfers between devices, body(): all_grad = lax.all_gather(hidden_grad, 'mp', axis=0, tiled=True)  145 us
    all_gather x1, waiting for transfers between devices, body(): all_inputs = lax.all_gather(inputs, 'dp', axis=0, tiled=True)  142 us
  transfers between devices with their start and end apart: 4, of which 4 were waited for; matrix products, arithmetic and copies ran while one was open for 1% of the time, Pallas kernels for 0%

commit v1 on v0

v1 whole, which is shorter than its diff:
```python
import functools
import math

import jax
import jax.numpy as jnp
from jax import lax
from jax.experimental import pallas as pl
from jax.experimental.pallas import tpu as pltpu
from jax.sharding import PartitionSpec as P

MESH = pl.DeviceIdType.MESH
F32, BF16 = jnp.float32, jnp.bfloat16
ROWS = 16


def gelu_slope(pre):
    cdf = 0.5 * (1.0 + lax.erf(pre * (1.0 / math.sqrt(2.0))))
    dens = jnp.exp(-0.5 * pre * pre) * (1.0 / math.sqrt(2.0 * math.pi))
    return cdf + pre * dens


def kernel(x_ref, a_ref, w_ref, b_ref, ig_ref, wg_ref, bg_ref,
           X, PA, RY, TY, Q, RZ, TZ, G, IG, RC, IX, RX, TX, K, RL, ssem, rsem):
    dp, mp = lax.axis_index("dp"), lax.axis_index("mp")
    zl, x, c = dp // 8, (dp // 2) % 4, dp % 2
    zh, y = mp // 4, mp % 4
    z0, zq, x1, x0 = zl % 2, zl // 2, x // 2, x % 2
    count = [0]
    sent = []

    def dev_zl(v):
        return (v * 8 + x * 2 + c, mp)

    def dev_x(v):
        return (zl * 8 + v * 2 + c, mp)

    def dev_y(v):
        return (dp, zh * 4 + v)

    def dev_z(v):
        return (dp, v * 4 + y)

    other = (zl * 8 + x * 2 + (1 - c), mp)

    def slot():
        count[0] += 1
        return count[0] - 1

    def send(src, dst, sem, dev):
        d = pltpu.make_async_remote_copy(
            src_ref=src, dst_ref=dst, send_sem=ssem.at[sem], recv_sem=rsem.at[sem],
            device_id=dev, device_id_type=MESH)
        d.start()
        sent.append(d)

    def landed(ref, sem):
        pltpu.make_async_remote_copy(
            src_ref=ref, dst_ref=ref, send_sem=ssem.at[sem], recv_sem=rsem.at[sem],
            device_id=other, device_id_type=MESH).wait_recv()

    def ag_start(me, dev, blk):
        up, down = (me + 1) % 4, (me + 3) % 4
        sems = [slot() for _ in range(6)]
        send(blk(me, 0), blk(me, 0), sems[0], dev(up))
        send(blk(me, 1), blk(me, 1), sems[3], dev(down))
        send(blk(me, 1), blk(me, 1), sems[1], dev(up))
        send(blk(me, 0), blk(me, 0), sems[4], dev(down))
        return sems

    def ag_forward(me, dev, blk, sems):
        up, down = (me + 1) % 4, (me + 3) % 4
        landed(blk(down, 0), sems[0])
        send(blk(down, 0), blk(down, 0), sems[2], dev(up))
        landed(blk(up, 1), sems[3])
        send(blk(up, 1), blk(up, 1), sems[5], dev(down))

    def ag_finish(me, blk, sems):
        up, down, far = (me + 1) % 4, (me + 3) % 4, (me + 2) % 4
        landed(blk(down, 1), sems[1])
        landed(blk(up, 0), sems[4])
        landed(blk(far, 0), sems[2])
        landed(blk(far, 1), sems[5])

    def rs_start(me, dev, blk, R):
        up, down, far = (me + 1) % 4, (me + 3) % 4, (me + 2) % 4
        sems = [slot() for _ in range(6)]
        send(blk(far, 0), R.at[0, 0], sems[0], dev(up))
        send(blk(far, 1), R.at[1, 0], sems[3], dev(down))
        send(blk(up, 1), R.at[0, 1], sems[1], dev(up))
        send(blk(down, 0), R.at[1, 1], sems[4], dev(down))
        return sems

    def rs_forward(me, dev, blk, R, T, sems):
        up, down = (me + 1) % 4, (me + 3) % 4
        landed(R.at[0, 0], sems[0])
        T[0] = (blk(up, 0)[...].astype(F32) + R[0, 0].astype(F32)).astype(BF16)
        send(T.at[0], R.at[0, 2], sems[2], dev(up))
        landed(R.at[1, 0], sems[3])
        T[1] = (blk(down, 1)[...].astype(F32) + R[1, 0].astype(F32)).astype(BF16)
        send(T.at[1], R.at[1, 2], sems[5], dev(down))

    def rs_finish(me, blk, R, sems):
        landed(R.at[1, 1], sems[4])
        landed(R.at[0, 1], sems[1])
        landed(R.at[0, 2], sems[2])
        landed(R.at[1, 2], sems[5])
        low = blk(me, 0)[...].astype(F32) + R[0, 2].astype(F32) + R[1, 1].astype(F32)
        high = blk(me, 1)[...].astype(F32) + R[1, 2].astype(F32) + R[0, 1].astype(F32)
        return low, high

    barrier = pltpu.get_barrier_semaphore()
    partners = [dev_zl((zl + d) % 8) for d in range(1, 8)]
    partners += [dev_x((x + 1) % 4), dev_x((x + 3) % 4)]
    partners += [dev_y((y + 1) % 4), dev_y((y + 3) % 4)]
    partners += [dev_z((zh + 1) % 4), dev_z((zh + 3) % 4), other]
    for p in partners:
        pl.semaphore_signal(barrier, inc=1, device_id=p, device_id_type=MESH)
    pl.semaphore_wait(barrier, len(partners))

    zsem = [slot() for _ in range(8)]
    for d in range(1, 8):
        send(x_ref, X.at[:, c, z0, x1, zq, x0], zsem[d], dev_zl((zl + d) % 8))
    X[:, c, z0, x1, zq, x0] = x_ref[...]
    for d in range(1, 8):
        s = (zl + 8 - d) % 8
        landed(X.at[:, c, s % 2, x1, s // 2, x0], zsem[d])

    def xblk(h):
        return lambda v, half: X.at[h, c, half, v // 2, :, v % 2]

    xs = [ag_start(x, dev_x, xblk(h)) for h in range(2)]
    for h in range(2):
        ag_forward(x, dev_x, xblk(h), xs[h])
    csem = [slot() for _ in range(2)]
    for h in range(2):
        ag_finish(x, xblk(h), xs[h])
        send(X.at[h, c], X.at[h, c], csem[h], other)

    def pblk(h):
        return lambda v, half: PA.at[h, half, v // 2, v % 2]

    ys = []
    for h in range(2):
        landed(X.at[h, 1 - c], csem[h])

        def pre_part(i, carry, h=h):
            rows = X[h, i // 2, i % 2].reshape(16 * ROWS, 384)
            part = jnp.dot(rows, w_ref[...], preferred_element_type=F32)
            PA[h, i // 2, i % 2] = part.astype(BF16).reshape(2, 4, 2, ROWS, 384)
            return carry

        lax.fori_loop(0, 4, pre_part, 0)
        ys.append(rs_start(y, dev_y, pblk(h), RY.at[h]))
    for h in range(2):
        rs_forward(y, dev_y, pblk(h), RY.at[h], TY.at[h], ys[h])

    def qblk(h):
        return lambda v, half: Q.at[h, half, v]

    zs = []
    for h in range(2):
        low, high = rs_finish(y, pblk(h), RY.at[h], ys[h])
        Q[h, 0] = low.astype(BF16)
        Q[h, 1] = high.astype(BF16)
        zs.append(rs_start(zh, dev_z, qblk(h), RZ.at[h]))
    for h in range(2):
        rs_forward(zh, dev_z, qblk(h), RZ.at[h], TZ.at[h], zs[h])

    def gz(h):
        return lambda v, half: G.at[h, half, y // 2, y % 2, v]

    def gy(h):
        return lambda v, half: G.at[h, half, v // 2, v % 2]

    gzs = []
    for h in range(2):
        sums = rs_finish(zh, qblk(h), RZ.at[h], zs[h])
        for half in range(2):
            for e in range(2):
                pre = sums[half][e] + b_ref[...]
                act = a_ref[pl.ds(32 * (2 * e + half) + ROWS * h, ROWS), :].astype(F32)
                G[h, half, y // 2, y % 2, zh, e] = (act * gelu_slope(pre)).astype(BF16)
        gzs.append(ag_start(zh, dev_z, gz(h)))
    for h in range(2):
        ag_forward(zh, dev_z, gz(h), gzs[h])
    gys = []
    for h in range(2):
        ag_finish(zh, gz(h), gzs[h])
        gys.append(ag_start(y, dev_y, gy(h)))
    for h in range(2):
        ag_forward(y, dev_y, gy(h), gys[h])

    isem = [slot() for _ in range(2)]
    for h in range(2):
        ag_finish(y, gy(h), gys[h])

        def ig_part(i, carry, h=h):
            rows = G[h, i // 2, i % 2].reshape(16 * ROWS, 384)
            part = lax.dot_general(rows, w_ref[...], (((1,), (1,)), ((), ())), preferred_element_type=F32)
            IG[h, i // 2, i % 2] = part.astype(BF16).reshape(2, 4, 2, ROWS, 384)
            return carry

        lax.fori_loop(0, 4, ig_part, 0)
        send(IG.at[h, 1 - c], RC.at[h], isem[h], other)

    def iblk(h):
        return lambda v, half: IX.at[h, half, v // 2, :, v % 2]

    ixs = []
    for h in range(2):
        landed(RC.at[h], isem[h])
        for half in range(2):
            IX[h, half] = (IG[h, c, half].astype(F32) + RC[h, half].astype(F32)).astype(BF16)
        ixs.append(rs_start(x, dev_x, iblk(h), RX.at[h]))
    for h in range(2):
        rs_forward(x, dev_x, iblk(h), RX.at[h], TX.at[h], ixs[h])
    lsems = []
    for h in range(2):
        low, high = rs_finish(x, iblk(h), RX.at[h], ixs[h])
        K[h, 0] = low.astype(BF16)
        K[h, 1] = high.astype(BF16)
        lsem = [slot() for _ in range(8)]
        lsems.append(lsem)
        for d in range(1, 8):
            t = (zl + d) % 8
            send(K.at[h, t % 2, t // 2], RL.at[h, d - 1], lsem[d], dev_zl(t))

    wg_ref[...] = jnp.zeros_like(wg_ref)
    bg_ref[...] = jnp.zeros_like(bg_ref)

    def wg_part(i, carry):
        h, j, k = i // 4, (i // 2) % 2, i % 2
        rows = G[h, j, k].reshape(16 * ROWS, 384)
        wg_ref[...] += lax.dot_general(
            X[h, j, k].reshape(16 * ROWS, 384), rows, (((0,), (0,)), ((), ())), preferred_element_type=F32)
        bg_ref[...] += jnp.sum(rows.astype(F32), axis=0, keepdims=True)
        return carry

    lax.fori_loop(0, 8, wg_part, 0)

    for h in range(2):
        total = K[h, z0, zq].astype(F32)
        for d in range(1, 8):
            landed(RL.at[h, d - 1], lsems[h][d])
            total = total + RL[h, d - 1].astype(F32)
        ig_ref[h] = total.astype(BF16)
    for d in sent:
        d.wait_send()


def body(inputs, act_grad, w_in, bias_in):
    vm = lambda *s: pltpu.VMEM(s, BF16)
    full = (2, 2, 2, 2, 4, 2, ROWS, 384)
    n = 140
    ig, wg, bg = pl.pallas_call(
        kernel,
        out_shape=(
            jax.ShapeDtypeStruct((2, ROWS, 384), BF16),
            jax.ShapeDtypeStruct((384, 384), F32),
            jax.ShapeDtypeStruct((1, 384), F32),
        ),
        in_specs=[pl.BlockSpec(memory_space=pltpu.VMEM)] * 4,
        out_specs=[pl.BlockSpec(memory_space=pltpu.VMEM)] * 3,
        scratch_shapes=[
            vm(*full),
            vm(*full),
            vm(2, 2, 3, 4, 2, ROWS, 384),
            vm(2, 2, 4, 2, ROWS, 384),
            vm(2, 2, 4, 2, ROWS, 384),
            vm(2, 2, 3, 2, ROWS, 384),
            vm(2, 2, 2, ROWS, 384),
            vm(*full),
            vm(*full),
            vm(2, 2, 2, 4, 2, ROWS, 384),
            vm(2, 2, 2, 4, 2, ROWS, 384),
            vm(2, 2, 3, 4, ROWS, 384),
            vm(2, 2, 4, ROWS, 384),
            vm(2, 2, 4, ROWS, 384),
            vm(2, 7, ROWS, 384),
            pltpu.SemaphoreType.DMA((n,)),
            pltpu.SemaphoreType.DMA((n,)),
        ],
        compiler_params=pltpu.CompilerParams(
            collective_id=0, has_side_effects=True, vmem_limit_bytes=48 * 1024 * 1024
        ),
    )(inputs.reshape(2, ROWS, 384), act_grad, w_in, bias_in.reshape(1, 384))
    return (ig.reshape(2 * ROWS, 384), wg, bg.reshape(384))


def solution(mesh):
    return jax.shard_map(
        body,
        mesh=mesh,
        in_specs=(P("dp", "mp"), P("mp", "dp"), P("mp", "dp"), P("dp")),
        out_specs=(P("dp", "mp"), P("mp", "dp"), P("dp")),
        check_vma=False,
    )
```

time: 951 us -> 163 us (0.17)
  waiting for transfers between devices: 912 us -> 0 us
  Pallas kernels: 0 us -> 156 us
  between operations: 13.8 us -> 0.64 us
  matrix products: 9.67 us -> 0 us
    reduce_scatter x2 -> x0, waiting for transfers between devices: 624 us -> none  [the longest x1 423 us: body(): lax.psum_scatter(contract(all_grad, w_in, 1, 1), 'dp', scatter_dimension=...]
    all_gather x2 -> x0, waiting for transfers between devices: 287 us -> none  [the longest x1 145 us: body(): all_grad = lax.all_gather(hidden_grad, 'mp', axis=0, tiled=True)]
    pallas_call x0 -> x1, Pallas kernels: none -> 156 us  [body(): pl.pallas_call(kernel, out_shape=(jax.ShapeDtypeStruct((2, ROWS, 384), BF...]
    dot_general x3 -> x0, matrix products: 9.67 us -> none  [contract(): lax.dot_general(left, right, (((left_dim,), (right_dim,)), ((), ())), pre...]
  transfers between devices with their start and end apart: 4 -> 0, of which waited for: 4 -> 0; matrix products, arithmetic and copies ran while one was open for 1% -> 0% of each run, Pallas kernels for 0% -> 0%
where the time goes in v1:
time: 163 us; the launch traced here: 162 us
  Pallas kernels  156 us (96%)
  local copies, waits for them, and re-layouts  4.7 us (3%)
    pallas_call x1, Pallas kernels, body(): pl.pallas_call(kernel, out_shape=(jax.ShapeDtypeStruct((2, ROWS, 384), BF...  156 us
    unnamed x8, local copies, waits for them, and re-layouts  4.01 us

profile of v1, /device:TPU:1, one launch (start us, length us, event | category | flops | bytes accessed | tf_op | source)
XLA Modules:
  0.0 161.9 jit_solution(11066678507936950224)
XLA Ops:
  0.6 0.7 reshape.19.b_ref
  1.3 0.0 copy-start
  1.3 1.0 copy-done
  2.3 0.0 copy-start.1
  2.3 0.9 copy-done.1
  3.2 0.0 copy-start.2
  3.2 0.7 copy-done.2
  3.9 156.0 %shard_map.67 = (bf16[2,16,384]{2,1,0:T(8,128)(2,1)S(1)}, f32[384,384]{1,0:T(8,128)S(1)}, f32[1,384]{1,0:T(1,128)S(1)}) custom-call(bf16[2,16,384]{2,1,0:T(8,128)(2,1)S(1)} %bitcast.2, bf16[128,384]{1,0:T(8,128)(2,1)S(1)} %copy-done.1, bf16[384,384]{1,0:T(8,128)(2,1)S(1)} %copy-done, f32[1,384]{1,0:T(1,128)S(1)} %reshape.19.b_ref), custom_call_target="tpu_custom_call" | custom-call | tf_op jit(solution)/shard_map/pallas_call | solution.py:255
  159.9 0.6 reduce
  160.5 0.6 copy.9
  161.1 0.8 copy.10
Async XLA Ops:
  1.3 1.0 copy-start
  2.3 0.9 copy-start.1
  3.2 0.7 copy-start.2

commit v2 on v0

v2 whole, which is shorter than its diff:
```python
import math

import jax
import jax.numpy as jnp
from jax import lax
from jax.experimental import pallas as pl
from jax.experimental.pallas import tpu as pltpu
from jax.sharding import PartitionSpec as P

MESH = pl.DeviceIdType.MESH
F32, BF16 = jnp.float32, jnp.bfloat16
ROWS = 16
CHUNKS = tuple((h, a, e) for h in range(2) for a in range(2) for e in range(2))
ORDER = (
    "zw0 zw1 xa0 b0 b1 xb0 b2 xa1 b3 b4 d0 xb1 b5 d1 b7 d2 b6 d3 d4 e0 d5 e1 d7 e2 d6 e3 e4 f0 e5 f1 e7 f2 f3 e6 f4 g0 f5 g1 g2 f7 g3 f6 g4 h0 g5 h1 h2 g7 j0 w0 h3 j1 w1 g6 j2 l0 h5 h4 w2 j3 h7 w3 l1 j5 h6 w5 j4 l2 w4 j7 n0 j6 l3 w6 w7 n1 o0 o1"
).split()


def gelu_slope(pre):
    cdf = 0.5 * (1.0 + lax.erf(pre * (1.0 / math.sqrt(2.0))))
    dens = jnp.exp(-0.5 * pre * pre) * (1.0 / math.sqrt(2.0 * math.pi))
    return cdf + pre * dens


def kernel(x_hbm, a_hbm, w_hbm, b_hbm, ig_ref, wg_ref, bg_ref,
           A, W, B, X, PA, RY, Q, RZ, TZ, G, IG, RC, IX, RX, K, RL, BG, lsem, ssem, rsem):
    dp, mp = lax.axis_index("dp"), lax.axis_index("mp")
    zl, x, c = dp // 8, (dp // 2) % 4, dp % 2
    zh, y = mp // 4, mp % 4
    z0, zq, x1, x0 = zl % 2, zl // 2, x // 2, x % 2
    count = [0]
    sent = []

    def dev_zl(v):
        return (v * 8 + x * 2 + c, mp)

    def dev_x(v):
        return (zl * 8 + v * 2 + c, mp)

    def dev_y(v):
        return (dp, zh * 4 + v)

    def dev_z(v):
        return (dp, v * 4 + y)

    other = (zl * 8 + x * 2 + (1 - c), mp)

    def slots(k):
        count[0] += k
        return list(range(count[0] - k, count[0]))

    def send(src, dst, sem, dev):
        d = pltpu.make_async_remote_copy(
            src_ref=src, dst_ref=dst, send_sem=ssem.at[sem], recv_sem=rsem.at[sem],
            device_id=dev, device_id_type=MESH)
        d.start()
        sent.append(d)

    def landed(ref, sem):
        pltpu.make_async_remote_copy(
            src_ref=ref, dst_ref=ref, send_sem=ssem.at[sem], recv_sem=rsem.at[sem],
            device_id=other, device_id_type=MESH).wait_recv()

    own = [
        pltpu.make_async_copy(w_hbm, W, lsem.at[0]),
        pltpu.make_async_copy(a_hbm, A, lsem.at[1]),
        pltpu.make_async_copy(b_hbm, B, lsem.at[2]),
    ]
    own += [
        pltpu.make_async_copy(
            x_hbm.at[pl.ds(h * ROWS, ROWS)], X.at[h, c, x0, z0, x1, zq], lsem.at[3 + h])
        for h in range(2)
    ]
    for d in own:
        d.start()

    barrier = pltpu.get_barrier_semaphore()
    partners = [dev_zl((zl + d) % 8) for d in range(1, 8)]
    partners += [dev_x((x + d) % 4) for d in range(1, 4)]
    partners += [dev_y((y + d) % 4) for d in range(1, 4)]
    partners += [dev_z((zh + 1) % 4), dev_z((zh + 3) % 4), other]
    for p in partners:
        pl.semaphore_signal(barrier, inc=1, device_id=p, device_id_type=MESH)
    for d in own:
        d.wait()
    pl.semaphore_wait(barrier, len(partners))

    s_in, s_x, s_core = [slots(8) for _ in range(2)], [slots(4) for _ in range(2)], [slots(2) for _ in range(2)]
    s_y, s_z = [slots(4) for _ in CHUNKS], [slots(3) for _ in CHUNKS]
    s_gz, s_gy = [slots(3) for _ in CHUNKS], [slots(4) for _ in CHUNKS]
    s_ic, s_ix, s_out = [slots(2) for _ in range(2)], [slots(4) for _ in range(2)], [slots(8) for _ in range(2)]

    def tok(q):
        h, a, e = CHUNKS[q]
        return h, (c if e == 0 else 1 - c), (x0 if a == 0 else 1 - x0)

    def ways(q):
        up, down = (zh + 1) % 4, (zh + 3) % 4
        return (up, down) if q % 2 == 0 else (down, up)

    def zw(h):
        for d in range(1, 8):
            s = (zl + 8 - d) % 8
            landed(X.at[h, c, x0, s % 2, x1, s // 2], s_in[h][d])
        mine = X.at[h, c, x0, :, x1]
        for d in (2, 1, 3):
            send(mine, mine, s_x[h][d], dev_x((x + d) % 4))

    def from_x(h, d):
        s = (x + 4 - d) % 4
        landed(X.at[h, c, s % 2, :, s // 2], s_x[h][d])

    def xa(h):
        from_x(h, 2)
        send(X.at[h, c, x0], X.at[h, c, x0], s_core[h][0], other)

    def xb(h):
        from_x(h, 1)
        from_x(h, 3)
        send(X.at[h, c, 1 - x0], X.at[h, c, 1 - x0], s_core[h][1], other)

    def b(q):
        h, t, s = tok(q)
        if CHUNKS[q][2] == 1:
            landed(X.at[h, t, s], s_core[h][CHUNKS[q][1]])
        out = jnp.dot(X[h, t, s].reshape(16 * ROWS, 384), W[...], preferred_element_type=F32)
        PA[q] = out.astype(BF16).reshape(4, 4, ROWS, 384)
        for d in (2, 1, 3):
            v = (y + d) % 4
            send(PA.at[q, v], RY.at[q, d - 1], s_y[q][d], dev_y(v))

    def d_(q):
        total = PA[q, y].astype(F32)
        for d in range(1, 4):
            landed(RY.at[q, d - 1], s_y[q][d])
            total = total + RY[q, d - 1].astype(F32)
        Q[q] = total.astype(BF16)
        first, second = ways(q)
        send(Q.at[q, (zh + 2) % 4], RZ.at[q, 0], s_z[q][0], dev_z(first))
        send(Q.at[q, second], RZ.at[q, 1], s_z[q][1], dev_z(second))

    def e_(q):
        first, second = ways(q)
        landed(RZ.at[q, 0], s_z[q][0])
        TZ[q] = (Q[q, first].astype(F32) + RZ[q, 0].astype(F32)).astype(BF16)
        send(TZ.at[q], RZ.at[q, 2], s_z[q][2], dev_z(first))

    def f_(q):
        h, t, s = tok(q)
        landed(RZ.at[q, 1], s_z[q][1])
        landed(RZ.at[q, 2], s_z[q][2])
        pre = Q[q, zh].astype(F32) + RZ[q, 1].astype(F32) + RZ[q, 2].astype(F32) + B[...].reshape(1, 384)
        row = pl.multiple_of(64 * s + 32 * t + ROWS * h, ROWS)
        act = A[pl.ds(row, ROWS), :].astype(F32)
        G[q, y, zh] = (act * gelu_slope(pre)).astype(BF16)
        first, second = ways(q)
        mine = G.at[q, y, zh]
        send(mine, mine, s_gz[q][0], dev_z(first))
        send(mine, mine, s_gz[q][1], dev_z(second))

    def g_(q):
        first, second = ways(q)
        landed(G.at[q, y, second], s_gz[q][0])
        send(G.at[q, y, second], G.at[q, y, second], s_gz[q][2], dev_z(first))

    def h_(q):
        first, second = ways(q)
        landed(G.at[q, y, first], s_gz[q][1])
        landed(G.at[q, y, (zh + 2) % 4], s_gz[q][2])
        for d in (2, 1, 3):
            send(G.at[q, y], G.at[q, y], s_gy[q][d], dev_y((y + d) % 4))

    def j_(q):
        h, a, e = CHUNKS[q]
        for d in range(1, 4):
            landed(G.at[q, (y + 4 - d) % 4], s_gy[q][d])
        out = lax.dot_general(
            G[q].reshape(16 * ROWS, 384), W[...], (((1,), (1,)), ((), ())), preferred_element_type=F32)
        IG[q] = out.astype(BF16).reshape(2, 2, 4, ROWS, 384)
        if e == 1:
            send(IG.at[q], RC.at[h, a], s_ic[h][a], other)

    def l_(k):
        h, a = k // 2, k % 2
        landed(RC.at[h, a], s_ic[h][a])
        both = IG[CHUNKS.index((h, a, 0))].astype(F32) + RC[h, a].astype(F32)
        for i in range(2):
            IX[h, a, i] = both[:, i].astype(BF16)
        for d in ((2,) if a == 0 else (1, 3)):
            v = (x + d) % 4
            send(IX.at[h, a, v // 2], RX.at[h, d - 1], s_ix[h][d], dev_x(v))

    def n_(h):
        total = IX[h, 0, x1].astype(F32)
        for d in range(1, 4):
            landed(RX.at[h, d - 1], s_ix[h][d])
            total = total + RX[h, d - 1].astype(F32)
        K[h] = total.astype(BF16)
        for d in range(1, 8):
            t = (zl + d) % 8
            send(K.at[h, t % 2, t // 2], RL.at[h, d - 1], s_out[h][d], dev_zl(t))

    def o_(h):
        total = K[h, z0, zq].astype(F32)
        for d in range(1, 8):
            landed(RL.at[h, d - 1], s_out[h][d])
            total = total + RL[h, d - 1].astype(F32)
        ig_ref[pl.ds(h * ROWS, ROWS), :] = total.astype(BF16)

    def w_(q):
        h, t, s = tok(q)
        rows = G[q].reshape(16 * ROWS, 384)
        wg_ref[...] += lax.dot_general(
            X[h, t, s].reshape(16 * ROWS, 384), rows, (((0,), (0,)), ((), ())), preferred_element_type=F32)
        BG[...] += jnp.sum(rows.astype(F32), axis=0, keepdims=True)

    for h in range(2):
        for d in range(1, 8):
            send(x_hbm.at[pl.ds(h * ROWS, ROWS)], X.at[h, c, x0, z0, x1, zq], s_in[h][d], dev_zl((zl + d) % 8))
    wg_ref[...] = jnp.zeros_like(wg_ref)
    BG[...] = jnp.zeros_like(BG)
    tasks = {"zw": zw, "xa": xa, "xb": xb, "b": b, "d": d_, "e": e_, "f": f_, "g": g_, "h": h_,
             "j": j_, "l": l_, "n": n_, "o": o_, "w": w_}
    for task in ORDER:
        tasks[task[:-1]](int(task[-1]))
    bg_ref[...] = BG[...].reshape(384)
    for d in sent:
        d.wait_send()


def body(inputs, act_grad, w_in, bias_in):
    vm = lambda *s: pltpu.VMEM(s, BF16)
    nq, n = len(CHUNKS), 180
    return pl.pallas_call(
        kernel,
        out_shape=(
            jax.ShapeDtypeStruct((2 * ROWS, 384), BF16),
            jax.ShapeDtypeStruct((384, 384), F32),
            jax.ShapeDtypeStruct((384,), F32),
        ),
        in_specs=[pl.BlockSpec(memory_space=pl.ANY)] * 4,
        out_specs=[pl.BlockSpec(memory_space=pltpu.VMEM)] * 3,
        scratch_shapes=[
            vm(128, 384),
            vm(384, 384),
            pltpu.VMEM((384,), F32),
            vm(2, 2, 2, 2, 2, 4, ROWS, 384),
            vm(nq, 4, 4, ROWS, 384),
            vm(nq, 3, 4, ROWS, 384),
            vm(nq, 4, ROWS, 384),
            vm(nq, 3, ROWS, 384),
            vm(nq, ROWS, 384),
            vm(nq, 4, 4, ROWS, 384),
            vm(nq, 2, 2, 4, ROWS, 384),
            vm(2, 2, 2, 2, 4, ROWS, 384),
            vm(2, 2, 2, 2, 4, ROWS, 384),
            vm(2, 3, 2, 4, ROWS, 384),
            vm(2, 2, 4, ROWS, 384),
            vm(2, 7, ROWS, 384),
            pltpu.VMEM((1, 384), F32),
            pltpu.SemaphoreType.DMA((5,)),
            pltpu.SemaphoreType.DMA((n,)),
            pltpu.SemaphoreType.DMA((n,)),
        ],
        compiler_params=pltpu.CompilerParams(
            collective_id=0, has_side_effects=True, vmem_limit_bytes=56 * 1024 * 1024
        ),
    )(inputs, act_grad, w_in, bias_in)


def solution(mesh):
    return jax.shard_map(
        body,
        mesh=mesh,
        in_specs=(P("dp", "mp"), P("mp", "dp"), P("mp", "dp"), P("dp")),
        out_specs=(P("dp", "mp"), P("mp", "dp"), P("dp")),
        check_vma=False,
    )
```

time: 951 us -> 136 us (0.14)
  waiting for transfers between devices: 912 us -> 0 us
  Pallas kernels: 0 us -> 131 us
  between operations: 13.8 us -> 0.64 us
  matrix products: 9.67 us -> 0 us
    reduce_scatter x2 -> x0, waiting for transfers between devices: 624 us -> none  [the longest x1 423 us: body(): lax.psum_scatter(contract(all_grad, w_in, 1, 1), 'dp', scatter_dimension=...]
    all_gather x2 -> x0, waiting for transfers between devices: 287 us -> none  [the longest x1 145 us: body(): all_grad = lax.all_gather(hidden_grad, 'mp', axis=0, tiled=True)]
    pallas_call x0 -> x1, Pallas kernels: none -> 131 us  [body(): pl.pallas_call(kernel, out_shape=(jax.ShapeDtypeStruct((2 * ROWS, 384), B...]
    dot_general x3 -> x0, matrix products: 9.67 us -> none  [contract(): lax.dot_general(left, right, (((left_dim,), (right_dim,)), ((), ())), pre...]
  transfers between devices with their start and end apart: 4 -> 0, of which waited for: 4 -> 0; matrix products, arithmetic and copies ran while one was open for 1% -> 0% of each run, Pallas kernels for 0% -> 0%
where the time goes in v2:
time: 136 us
  Pallas kernels  131 us (96%)
  local copies, waits for them, and re-layouts  3.85 us (3%)
    pallas_call x1, Pallas kernels, body(): pl.pallas_call(kernel, out_shape=(jax.ShapeDtypeStruct((2 * ROWS, 384), B...  131 us
    unnamed x5, local copies, waits for them, and re-layouts  3.85 us

profile of v2, /device:TPU:1, one launch (start us, length us, event | category | flops | bytes accessed | tf_op | source)
XLA Modules:
  0.0 135.8 jit_solution(2070984574282149990)
XLA Ops:
  0.6 131.3 %shard_map.67 = (bf16[32,384]{1,0:T(8,128)(2,1)}, f32[384,384]{1,0:T(8,128)}, f32[384]{0:T(512)}) custom-call(bf16[32,384]{1,0:T(8,128)(2,1)} %x_hbm.1, bf16[128,384]{1,0:T(8,128)(2,1)} %a_hbm.1, bf16[384,384]{1,0:T(8,128)(2,1)} %w_hbm.1, f32[384]{0:T(512)} %b_hbm.1), custom_call_target="tpu_custom_call" | custom-call | tf_op jit(solution)/shard_map/pallas_call | solution.py:234
  131.9 1.3 copy.10
  133.3 0.0 copy-start
  133.3 1.9 %copy.11 = f32[384,384]{1,0:T(8,128)} copy(f32[384,384]{1,0:T(8,128)} %get-tuple-element.7) | data formatting | bytes 1179648
  135.2 0.0 copy-done
  135.2 0.6 copy.12
Async XLA Ops:
  133.3 1.9 %copy-start = (f32[384]{0:T(512)S(1)}, f32[384]{0:T(512)}, u32[]{:S(2)}) copy-start(f32[384]{0:T(512)} %get-tuple-element.8) | copy-start | bytes 4612

commit v3 on v2

--- a/solution.py
+++ b/solution.py
@@ -12,7 +12,7 @@
 ROWS = 16
 CHUNKS = tuple((h, a, e) for h in range(2) for a in range(2) for e in range(2))
 ORDER = (
-    "zw0 zw1 xa0 b0 b1 xb0 b2 xa1 b3 b4 d0 xb1 b5 d1 b7 d2 b6 d3 d4 e0 d5 e1 d7 e2 d6 e3 e4 f0 e5 f1 e7 f2 f3 e6 f4 g0 f5 g1 g2 f7 g3 f6 g4 h0 g5 h1 h2 g7 j0 w0 h3 j1 w1 g6 j2 l0 h5 h4 w2 j3 h7 w3 l1 j5 h6 w5 j4 l2 w4 j7 n0 j6 l3 w6 w7 n1 o0 o1"
+    "zw0 zs1 xa0 b0 zw1 b1 xb0 b2 xa1 b4 d0 xb1 b5 d1 b3 d2 b6 d4 b7 e0 d5 d3 e1 d6 e2 d7 f0 e3 f1 e7 e5 f2 e6 g0 f3 g1 f7 e4 h0 f5 g3 f6 g2 h1 g7 f4 j1 g6 g5 h3 w1 h2 j0 w0 g4 h7 j3 h6 j2 h5 w2 j7 l1 h4 l0 w3 j6 l3 j5 w5 j4 l2 n0 w6 w7 n1 w4 o0 o1"
 ).split()
 
 
@@ -214,18 +214,21 @@
             X[h, t, s].reshape(16 * ROWS, 384), rows, (((0,), (0,)), ((), ())), preferred_element_type=F32)
         BG[...] += jnp.sum(rows.astype(F32), axis=0, keepdims=True)
 
-    for h in range(2):
+    def zs(h):
         for d in range(1, 8):
             send(x_hbm.at[pl.ds(h * ROWS, ROWS)], X.at[h, c, x0, z0, x1, zq], s_in[h][d], dev_zl((zl + d) % 8))
+
+    zs(0)
     wg_ref[...] = jnp.zeros_like(wg_ref)
     BG[...] = jnp.zeros_like(BG)
-    tasks = {"zw": zw, "xa": xa, "xb": xb, "b": b, "d": d_, "e": e_, "f": f_, "g": g_, "h": h_,
+    tasks = {"zs": zs, "zw": zw, "xa": xa, "xb": xb, "b": b, "d": d_, "e": e_, "f": f_, "g": g_, "h": h_,
              "j": j_, "l": l_, "n": n_, "o": o_, "w": w_}
-    for task in ORDER:
+    for task in ORDER[:-1]:
         tasks[task[:-1]](int(task[-1]))
     bg_ref[...] = BG[...].reshape(384)
     for d in sent:
         d.wait_send()
+    tasks[ORDER[-1][:-1]](int(ORDER[-1][-1]))
 
 
 def body(inputs, act_grad, w_in, bias_in):

time: 136 us -> 134 us (0.985); the launches traced: 136 us -> 132 us
  Pallas kernels: 131 us -> 128 us
    pallas_call x1, Pallas kernels: 131 us -> 128 us  [body(): pl.pallas_call(kernel, out_shape=(jax.ShapeDtypeStruct((2 * ROWS, 384), B...]
where the time goes in v3:
time: 134 us; the launch traced here: 132 us
  Pallas kernels  128 us (96%)
  local copies, waits for them, and re-layouts  3.85 us (3%)
    pallas_call x1, Pallas kernels, body(): pl.pallas_call(kernel, out_shape=(jax.ShapeDtypeStruct((2 * ROWS, 384), B...  128 us
    unnamed x5, local copies, waits for them, and re-layouts  3.85 us

profile of v3, /device:TPU:1, one launch (start us, length us, event | category | flops | bytes accessed | tf_op | source)
XLA Modules:
  0.0 132.2 jit_solution(18431932120812211121)
XLA Ops:
  0.6 127.7 %shard_map.67 = (bf16[32,384]{1,0:T(8,128)(2,1)}, f32[384,384]{1,0:T(8,128)}, f32[384]{0:T(512)}) custom-call(bf16[32,384]{1,0:T(8,128)(2,1)} %x_hbm.1, bf16[128,384]{1,0:T(8,128)(2,1)} %a_hbm.1, bf16[384,384]{1,0:T(8,128)(2,1)} %w_hbm.1, f32[384]{0:T(512)} %b_hbm.1), custom_call_target="tpu_custom_call" | custom-call | tf_op jit(solution)/shard_map/pallas_call | solution.py:237
  128.3 1.3 %copy.10 = bf16[32,384]{1,0:T(8,128)(2,1)} copy(bf16[32,384]{1,0:T(8,128)(2,1)} %get-tuple-element.6) | data formatting | bytes 49152
  129.7 0.0 copy-start
  129.7 1.9 %copy.11 = f32[384,384]{1,0:T(8,128)} copy(f32[384,384]{1,0:T(8,128)} %get-tuple-element.7) | data formatting | bytes 1179648
  131.6 0.0 copy-done
  131.6 0.6 copy.12
Async XLA Ops:
  129.7 1.9 %copy-start = (f32[384]{0:T(512)S(1)}, f32[384]{0:T(512)}, u32[]{:S(2)}) copy-start(f32[384]{0:T(512)} %get-tuple-element.8) | copy-start | bytes 4612

commit v4 on v3

--- a/solution.py
+++ b/solution.py
@@ -12,7 +12,7 @@
 ROWS = 16
 CHUNKS = tuple((h, a, e) for h in range(2) for a in range(2) for e in range(2))
 ORDER = (
-    "zw0 zs1 xa0 b0 zw1 b1 xb0 b2 xa1 b4 d0 xb1 b5 d1 b3 d2 b6 d4 b7 e0 d5 d3 e1 d6 e2 d7 f0 e3 f1 e7 e5 f2 e6 g0 f3 g1 f7 e4 h0 f5 g3 f6 g2 h1 g7 f4 j1 g6 g5 h3 w1 h2 j0 w0 g4 h7 j3 h6 j2 h5 w2 j7 l1 h4 l0 w3 j6 l3 j5 w5 j4 l2 n0 w6 w7 n1 w4 o0 o1"
+    "zw0 zs1 xa0 b0 zw1 b1 xa1 b4 xb0 b2 d0 xb1 b5 d1 b3 d2 b6 d4 b7 e0 d5 d3 e1 d6 e2 d7 f0 e3 f1 e7 e5 f2 e6 g0 f3 g1 f7 e4 h0 f5 g3 f6 g2 h1 g7 f4 j1 g6 g5 h3 w1 h2 j0 l0 w0 g4 h7 j3 h6 j2 l1 h5 w2 j7 h4 n0 j6 l3 j5 j4 l2 n1 w3 w5 w6 w7 w4 o0 o1"
 ).split()
 
 

time: 134 us -> 134 us (level); the launches traced: 132 us -> 134 us
    pallas_call x1, Pallas kernels: 128 us -> 129 us  [body(): pl.pallas_call(kernel, out_shape=(jax.ShapeDtypeStruct((2 * ROWS, 384), B...]
where the time goes in v4:
time: 134 us
  Pallas kernels  129 us (96%)
  local copies, waits for them, and re-layouts  3.85 us (3%)
    pallas_call x1, Pallas kernels, body(): pl.pallas_call(kernel, out_shape=(jax.ShapeDtypeStruct((2 * ROWS, 384), B...  129 us
    unnamed x5, local copies, waits for them, and re-layouts  3.85 us

profile of v4, /device:TPU:1, one launch (start us, length us, event | category | flops | bytes accessed | tf_op | source)
XLA Modules:
  0.0 133.6 jit_solution(5578136187382046426)
XLA Ops:
  0.6 129.1 %shard_map.67 = (bf16[32,384]{1,0:T(8,128)(2,1)}, f32[384,384]{1,0:T(8,128)}, f32[384]{0:T(512)}) custom-call(bf16[32,384]{1,0:T(8,128)(2,1)} %x_hbm.1, bf16[128,384]{1,0:T(8,128)(2,1)} %a_hbm.1, bf16[384,384]{1,0:T(8,128)(2,1)} %w_hbm.1, f32[384]{0:T(512)} %b_hbm.1), custom_call_target="tpu_custom_call" | custom-call | tf_op jit(solution)/shard_map/pallas_call | solution.py:237
  129.7 1.3 %copy.10 = bf16[32,384]{1,0:T(8,128)(2,1)} copy(bf16[32,384]{1,0:T(8,128)(2,1)} %get-tuple-element.6) | data formatting | bytes 49152
  131.1 0.0 copy-start
  131.1 1.9 %copy.11 = f32[384,384]{1,0:T(8,128)} copy(f32[384,384]{1,0:T(8,128)} %get-tuple-element.7) | data formatting | bytes 1179648
  133.0 0.0 copy-done
  133.0 0.6 copy.12
Async XLA Ops:
  131.1 1.9 %copy-start = (f32[384]{0:T(512)S(1)}, f32[384]{0:T(512)}, u32[]{:S(2)}) copy-start(f32[384]{0:T(512)} %get-tuple-element.8) | copy-start | bytes 4612
